TPU v7x, 32 devices: a whole 2x2x4 slice. The times are simulated.
32 devices in a mesh: sp: 8 (over z, y), tp: 4 (over x, core).
Axes of the slice: x: 2, y: 2, z: 4, core: 2. Of those that a mesh axis runs over, the one named last changes fastest.
Arguments:
- inputs: bfloat16 [25088, 1024], P(('sp', 'tp')), may hold values from -100 to 100, as said below
- grad_out: bfloat16 [25088, 512], P(('sp', 'tp')), may hold values from -6 to 6
- window_valid: int32 [512], P('sp'), may hold values 0 or 1
- window_edge: int32 [512], P('sp'), may hold values from 0 to 3
- merge_gain: bfloat16 [1024], replicated, may hold values from 0.5 to 1.5
- merge_bias: bfloat16 [1024], replicated, may hold values from -1.75 to 1.75
- merge_weight: bfloat16 [1024, 512], P(None, 'tp'), may hold values from -0.1875 to 0.1875
- attn_gain: bfloat16 [512], replicated, may hold values from 0.5 to 1.5
- attn_bias: bfloat16 [512], replicated, may hold values from -1.75 to 1.75
- query_key_value_weight: bfloat16 [512, 3, 512], P(None, None, 'tp'), may hold values from -0.25 to 0.25
- qv_bias: bfloat16 [2, 512], P(None, 'tp'), may hold values from -1.75 to 1.75
- rel_table: bfloat16 [169, 16], P(None, 'tp'), may hold values from -6 to 6
- proj_weight: bfloat16 [512, 512], P('tp'), may hold values from -0.75 to 0.75
- proj_bias: bfloat16 [512], replicated, may hold values from -1.75 to 1.75
- mlp_gain: bfloat16 [512], replicated, may hold values from 0.5 to 1.5
- mlp_bias: bfloat16 [512], replicated, may hold values from -1.75 to 1.75
- up_weight: bfloat16 [512, 2048], P(None, 'tp'), may hold values from -0.25 to 0.25
- up_bias: bfloat16 [2048], P('tp'), may hold values from -1.75 to 1.75
- down_weight: bfloat16 [2048, 512], P('tp'), may hold values from -0.125 to 0.125
- down_bias: bfloat16 [512], replicated, may hold values from -1.75 to 1.75
Outputs:
- block_out: bfloat16 [25088, 512], P(('sp', 'tp'))
- grad_inputs: float32 [25088, 1024], P(('sp', 'tp'))
- grad_merge_gain: float32 [1024], replicated
- grad_merge_bias: float32 [1024], replicated
- grad_merge_weight: float32 [1024, 512], P(None, 'tp')
- grad_attn_gain: float32 [512], replicated
- grad_attn_bias: float32 [512], replicated
- grad_qkv_weight: float32 [512, 3, 512], P(None, None, 'tp')
- grad_qv_bias: float32 [2, 512], P(None, 'tp')
- grad_rel_table: float32 [169, 16], P(None, 'tp')
- grad_proj_weight: float32 [512, 512], P('tp')
- grad_proj_bias: float32 [512], replicated
- grad_mlp_gain: float32 [512], replicated
- grad_mlp_bias: float32 [512], replicated
- grad_up_weight: float32 [512, 2048], P(None, 'tp')
- grad_up_bias: float32 [2048], P('tp')
- grad_down_weight: float32 [2048, 512], P('tp')
- grad_down_bias: float32 [512], replicated
Inputs may be any that keep to these rules, and one draw needn't show every extreme that they name: `inputs`: section-2 features; each feature has its own scale and each token its own. `window_edge`: bit 0 set: the window's last three columns come from the page's other side under the shift; bit 1: the same for its last three rows. `window_valid`: 0 marks a window of a padded page area.
All inputs are finite; a program needn't handle non-finite values. No bound on the sum of `window_valid` on one device may be relied on, other than what follows from the above.
Results may differ from a plain program's by a relative error of at most 0.02.
Values may be sent and summed in bfloat16 or wider, within the bound.
A program may use at most 128 MiB of HBM per device.

v0:
```python
import functools
import math

import jax
import jax.numpy as jnp
from jax import lax
from jax.experimental import pallas as pl
from jax.experimental.pallas import tpu as pltpu
from jax.sharding import PartitionSpec as P

SIDE = 7
TOK = SIDE * SIDE
REL_SIDE = 2 * SIDE - 1
REL = REL_SIDE * REL_SIDE
SPAN = 64
GROUP = 4
HD = 32
LANES = 128
EPSILON = 1e-05
NEG_FILL = -1000000000.0
MIB = 1 << 20
F32 = jnp.float32
BF16 = jnp.bfloat16


def dot(left, right):
    return jnp.dot(left, right, preferred_element_type=F32)


def dot_cols(left, right):
    return lax.dot_general(left, right, (((1,), (1,)), ((), ())), preferred_element_type=F32)


def dot_rows(left, right):
    return lax.dot_general(left, right, (((0,), (0,)), ((), ())), preferred_element_type=F32)


def rows_at(index, size):
    return pl.ds(pl.multiple_of(index * size, size), size)


def each(count, body, unroll=1):
    def step(index, carry):
        body(index)
        return carry

    lax.fori_loop(0, count, step, 0, unroll=unroll)


def fold(values):
    total = values[0:8]
    for start in range(8, values.shape[0], 8):
        total = total + values[start : start + 8]
    return total


def iota(shape, dim):
    return lax.broadcasted_iota(jnp.int32, shape, dim)


def norm_rows(values):
    mean = jnp.mean(values, -1, keepdims=True)
    centred = values - mean
    inv = lax.rsqrt(jnp.mean(centred * centred, -1, keepdims=True) + EPSILON)
    return centred * inv, mean, inv


def norm_back(upstream, normed, inv, gain):
    scaled = upstream * gain
    return inv * (
        scaled
        - jnp.mean(scaled, -1, keepdims=True)
        - normed * jnp.mean(scaled * normed, -1, keepdims=True)
    )


def gelu_both(values):
    bell = jnp.exp2(values * values * -0.7213475204444817)
    span = 1.0 + 0.23164190 * jnp.abs(values)
    t = pltpu.reciprocal(span, approx=True)
    t = t * (2.0 - span * t)
    poly = t * (
        0.127414796
        + t * (-0.142248368 + t * (0.7107068705 + t * (-0.7265760135 + t * 0.5307027145)))
    )
    tail = poly * bell
    phi = jnp.where(values >= 0, 1.0 - tail, tail)
    return values * phi, phi + values * bell * 0.3989422804014327


def window_row_col(index):
    row = (index * 37) >> 8
    return row, index - SIDE * row


def region_ids(index, edge, outside):
    row, col = window_row_col(index)
    high = SIDE - SIDE // 2
    region = (edge & 1) * (col >= high).astype(jnp.int32) + 2 * (edge >> 1) * (
        row >= high
    ).astype(jnp.int32)
    return jnp.where((index >= 0) & (index < TOK), region, outside)


def head_masks():
    lane = iota((1, LANES), 1)
    return [((lane >> 5) == head).astype(F32).astype(BF16) for head in range(GROUP)]


def spread_heads(block, masks):
    return jnp.concatenate([block * mask for mask in masks], axis=0)


def pick_heads(product):
    lane = iota((SPAN, LANES), 1)
    result = product[3 * SPAN : 4 * SPAN]
    for head in (2, 1, 0):
        result = jnp.where(
            lane < (head + 1) * HD, product[head * SPAN : (head + 1) * SPAN], result
        )
    return result


def same_head(rows, columns):
    return (
        (iota((rows, columns), 0) // (rows // GROUP))
        == (iota((rows, columns), 1) // (columns // GROUP))
    ).astype(F32).astype(BF16)


def offset_select(half):
    place = iota((LANES, LANES), 0)
    lane = iota((LANES, LANES), 1)
    token = lane - half * SPAN
    row, col = window_row_col(token & (SPAN - 1))
    wanted = (SIDE - 1) * (REL_SIDE + 1) - (REL_SIDE * row + col)
    hit = (place == wanted) & (token >= 0) & (token < TOK)
    return hit.astype(F32).astype(BF16)


def build_bias(table, spread_ref, bias_ref):
    heads = table.shape[0]

    def one(index):
        row = index // SIDE
        shift = index + (SIDE - 1) * row
        rolled = pltpu.roll(table, (2 * LANES - shift) % (2 * LANES), 1)
        spread_ref[rows_at(index, heads), :] = rolled[:, :LANES]

    spread_ref[...] = jnp.zeros_like(spread_ref)
    for index in range(TOK):
        one(index)
    low, high = offset_select(0), offset_select(1)
    for pair in range(heads // 2):
        first = spread_ref[pl.ds(2 * pair, SPAN, stride=heads), :].astype(BF16)
        second = spread_ref[pl.ds(2 * pair + 1, SPAN, stride=heads), :].astype(BF16)
        bias_ref[:, pair * LANES : (pair + 1) * LANES] = dot(first, low) + dot(second, high)


def split_bf16(values):
    high = values.astype(BF16)
    return high, (values - high.astype(F32)).astype(BF16)


def reduce_bias(bias_ref, spread_ref, heads):
    low, high = offset_select(0), offset_select(1)
    for pair in range(heads // 2):
        parts = split_bf16(bias_ref[:, pair * LANES : (pair + 1) * LANES])
        spread_ref[pl.ds(2 * pair, SPAN, stride=heads), :] = sum(
            dot_cols(part, low) for part in parts
        )
        spread_ref[pl.ds(2 * pair + 1, SPAN, stride=heads), :] = sum(
            dot_cols(part, high) for part in parts
        )
    total = jnp.zeros((heads, 2 * LANES), F32)
    blank = jnp.zeros((heads, LANES), F32)
    for index in range(TOK):
        shift = index + (SIDE - 1) * (index // SIDE)
        row = jnp.concatenate([spread_ref[index * heads : (index + 1) * heads, :], blank], axis=1)
        total = total + (pltpu.roll(row, shift, 1) if shift else row)
    return total


def shift_both(ref, forward):
    rows, columns = ref.shape
    down, right = (1, 1) if forward else (rows - 1, columns - 1)
    ref[...] = pltpu.roll(pltpu.roll(ref[...], down, 0), right, 1)


def attention_forward(first, edges, qkv, bias_ref, probs_ref, att_ref):
    masks = head_masks()
    size = GROUP * SPAN
    ones = same_head(size, size)
    first_half = iota((SPAN, LANES), 1) < SPAN
    groups = range(att_ref.shape[1] // LANES)

    def part_of(array, group, width):
        return array[:, group * width : (group + 1) * width]

    def tops(values):
        found = []
        for half in range(size // LANES):
            piece = part_of(values, half, LANES)
            low = jnp.max(jnp.where(first_half, piece, 2 * NEG_FILL), -1, keepdims=True)
            high = jnp.max(jnp.where(first_half, 2 * NEG_FILL, piece), -1, keepdims=True)
            found.append(jnp.where(first_half, low, high))
        return jnp.concatenate(found, axis=1)

    bias = bias_ref[...]
    states = []
    for index, edge in enumerate(edges):
        window = first + index
        base = pl.ds(pl.multiple_of(window * (TOK - 1), 16), SPAN)
        row_index = iota((SPAN, 1), 0) - window
        row_in = (row_index >= 0) & (row_index < TOK)
        row_region = region_ids(row_index, edge, 8)
        lane_region = region_ids((iota((1, size), 1) & (SPAN - 1)) - window, edge, 16)
        query, key, value = (qkv[part, base, :] for part in range(3))
        states.append((window, base, row_in, row_region == lane_region, query, key, value, bias))
        bias = pltpu.roll(pltpu.roll(bias, 1, 0), 1, 1)
    bias_ref[...] = bias

    logits = [
        [
            jnp.where(
                allowed,
                dot_cols(
                    part_of(query, group, LANES), spread_heads(part_of(key, group, LANES), masks)
                )
                * (HD**-0.5)
                + part_of(shifted, group, size),
                NEG_FILL,
            )
            for group in groups
        ]
        for _, _, _, allowed, query, key, _, shifted in states
    ]
    terms = [[jnp.exp(values - tops(values)) for values in row] for row in logits]
    totals = [[dot(values.astype(BF16), ones) for values in row] for row in terms]
    probs = [
        [
            (terms[index][group] * (state[2].astype(F32) / totals[index][group])).astype(BF16)
            for group in groups
        ]
        for index, state in enumerate(states)
    ]
    attended = [
        jnp.concatenate(
            [
                dot(probs[index][group], spread_heads(part_of(state[6], group, LANES), masks))
                for group in groups
            ],
            axis=1,
        )
        for index, state in enumerate(states)
    ]
    for index, (window, base, row_in, *_) in enumerate(states):
        for group in groups:
            probs_ref[window, :, pl.ds(group * size, size)] = probs[index][group]
        before = att_ref[base, :].astype(F32)
        att_ref[base, :] = jnp.where(row_in, attended[index], before).astype(BF16)


def attention_backward(windows, qkv, d_att, probs_ref, d_bias_ref, d_qkv):
    masks = head_masks()
    size = GROUP * SPAN
    ones = same_head(size, size)
    groups = range(d_att.shape[1] // LANES)
    factor = HD**-0.5

    def part_of(array, group, width):
        return array[:, group * width : (group + 1) * width]

    states = []
    for window in windows:
        base = pl.ds(pl.multiple_of(window * (TOK - 1), 16), SPAN)
        query, key, value = (qkv[part, base, :] for part in range(3))
        states.append((base, query, key, value, d_att[base, :], probs_ref[window]))
    d_bias = d_bias_ref[...]

    weighted = [
        [
            dot_cols(
                part_of(upstream, group, LANES),
                spread_heads(part_of(value, group, LANES), masks),
            )
            * part_of(probs, group, size).astype(F32)
            for group in groups
        ]
        for _, _, _, value, upstream, probs in states
    ]
    deltas = [[dot(values.astype(BF16), ones) for values in row] for row in weighted]
    d_logits = [
        [
            (
                weighted[index][group]
                - part_of(state[5], group, size).astype(F32) * deltas[index][group]
            ).astype(BF16)
            for group in groups
        ]
        for index, state in enumerate(states)
    ]
    for row in d_logits:
        d_bias = pltpu.roll(pltpu.roll(d_bias, SPAN - 1, 0), d_bias.shape[1] - 1, 1)
        d_bias = d_bias + jnp.concatenate([values.astype(F32) for values in row], axis=1)
    d_bias_ref[...] = d_bias
    results = []
    for index, (base, query, key, value, upstream, probs) in enumerate(states):
        row = d_logits[index]
        d_query = [
            dot(row[group], spread_heads(part_of(key, group, LANES), masks)) * factor
            for group in groups
        ]
        d_key = [
            pick_heads(dot_rows(row[group], part_of(query, group, LANES))) * factor
            for group in groups
        ]
        d_value = [
            pick_heads(dot_rows(part_of(probs, group, size), part_of(upstream, group, LANES)))
            for group in groups
        ]
        results.append([jnp.concatenate(values, axis=1) for values in (d_query, d_key, d_value)])
    for index, window in enumerate(windows):
        base = states[index][0]
        row_index = iota((SPAN, 1), 0) - window
        row_in = (row_index >= 0) & (row_index < TOK)
        for part in range(3):
            old = d_qkv[part, base, :].astype(F32)
            d_qkv[part, base, :] = jnp.where(row_in, results[index][part], old).astype(BF16)


def sum_rows(values):
    return jnp.sum(values, 0, keepdims=True)


class Local:
    def __init__(self, refs, first_window):
        self.__dict__.update(refs)
        self.first_window = first_window
        self.rows, self.wide = self.x.shape
        self.width = self.section.shape[1]
        self.units = self.hidden.shape[1]
        self.windows = self.rows // TOK
        self.heads = self.width // HD
        self.chunk = self.rows
        self.steps = self.rows // self.chunk
        self.tile = self.units // self.gu.shape[0]

    def gain(self, row, lanes):
        return self.gains[row : row + 1, :lanes]

    def stat(self, at, index):
        return self.stats[at, index : index + 1]

    def keep_stats(self, at, index, mean, inv):
        self.stats[at, index : index + 1] = mean
        self.stats[at, index + 1 : index + 2] = inv

    def tiles(self):
        return [lax.axis_index("tp") ^ bits for bits in (3, 2, 1, 0)]

    def begin(self):
        for copy in self.arriving:
            copy.wait()
        self.early[...] = jnp.zeros_like(self.early)
        self.spread_vectors()

    def spread_vectors(self):
        for row, ref in enumerate(self.vectors):
            values = ref[...].astype(F32)
            for block in range(values.shape[0]):
                lanes = slice(block * LANES, (block + 1) * LANES)
                self.gains[row : row + 1, lanes] = values[block : block + 1]

    def prepare(self):
        def keep_rows(window):
            base = pl.ds(pl.multiple_of(window * (TOK - 1), 16), SPAN)
            index = iota((SPAN, 1), 0) - window
            inside = (index >= 0) & (index < TOK)
            valid = self.valid[self.first_window + window].astype(F32)
            self.stats[base, 6:7] = jnp.where(inside, valid, self.stats[base, 6:7])

        each(self.windows, keep_rows)

    def table_bias(self):
        build_bias(self.table(), self.spread, self.bias)

    def merge_norm(self):
        gain, shift = self.gain(0, self.wide), self.gain(1, self.wide)

        def step(index):
            at = rows_at(index, self.chunk)
            normed, mean, inv = norm_rows(self.x[at, :].astype(F32))
            self.merged[at, :] = (normed * gain + shift).astype(BF16)
            self.keep_stats(at, 0, mean, inv)

        each(self.steps, step)

    def merge(self):
        self.section[...] = dot(self.merged[...], self.wm[...]).astype(BF16)

    def attn_norm(self):
        gain, shift = self.gain(2, self.width), self.gain(3, self.width)

        def step(index):
            at = rows_at(index, self.chunk)
            normed, mean, inv = norm_rows(self.section[at, :].astype(F32))
            self.attn_in[at, :] = (normed * gain + shift).astype(BF16)
            self.keep_stats(at, 2, mean, inv)

        each(self.steps, step)

    def project(self, part):
        product = dot(self.attn_in[...], self.wqkv[part])
        if part != 1:
            product = product + self.qkv_bias(part)
        self.qkv[part] = product.astype(BF16)

    def attend(self, first, last, together=4):
        def step(index):
            window = first + index * together
            edges = [self.edge[self.first_window + window + more] for more in range(together)]
            attention_forward(window, edges, self.qkv, self.bias, self.probs, self.att)

        each((last - first) // together, step)

    def attn_out(self):
        self.pre[...] = dot(self.att[...], self.wp[...])

    def mlp_norm(self):
        gain, shift = self.gain(4, self.width), self.gain(5, self.width)
        proj_bias = self.gain(6, self.width)

        def step(index):
            at = rows_at(index, self.chunk)
            total = self.section[at, :].astype(F32) + self.pre[at, :] + proj_bias
            self.resid[at, :] = total
            normed, mean, inv = norm_rows(total)
            self.mlp_in[at, :] = (normed * gain + shift).astype(BF16)
            self.keep_stats(at, 4, mean, inv)

        each(self.steps, step)

    def up(self, index):
        columns = rows_at(index, self.tile)
        self.pre[...] = dot(self.mlp_in[...], self.wu[:, columns])
        shift = self.up_bias(index)

        def activate(step):
            at = rows_at(step, self.rows // 7)
            value, rate = gelu_both(self.pre[at, :] + shift)
            self.hidden[at, columns] = value.astype(BF16)
            self.slope[at, columns] = rate.astype(BF16)

        each(7, activate)
        put_blocks(self.gd, index, dot_rows(self.hidden[:, columns], self.d_mlp[...]))

    def down(self):
        self.pre[...] = dot(self.hidden[...], self.wd[...])

    def grad_rows(self):
        def step(index, total):
            at = rows_at(index, self.chunk)
            grad = self.grad_out[at, :].astype(F32) * self.stat(at, 6)
            self.d_mlp[at, :] = grad.astype(BF16)
            return total + fold(grad)

        total = lax.fori_loop(
            0, self.steps, step, jnp.zeros((8, self.width), F32)
        )
        self.put_sum(7, total)

    def finish(self):
        down_bias = self.gain(7, self.width)

        def step(index):
            at = rows_at(index, self.chunk)
            block = (self.resid[at, :] + self.pre[at, :] + down_bias) * self.stat(at, 6)
            self.out[at, :] = block.astype(BF16)

        each(self.steps, step)

    def hidden_back(self, index):
        columns = rows_at(index, self.tile)
        slope = self.slope[:, columns].astype(F32)
        grad = (dot_cols(self.d_mlp[...], self.wd[columns, :]) * slope).astype(BF16)
        self.d_pre[:, columns] = grad
        self.put_up_sum(index, fold(grad.astype(F32)))
        put_blocks(self.gu, index, dot_rows(self.mlp_in[...], grad))

    def hidden_back_pair(self):
        each(2, lambda index: self.hidden_back(lax.axis_index("tp") ^ (2 - index)))

    def up_back(self):
        self.pre[...] = dot_cols(self.d_pre[...], self.wu[...])

    def mlp_back(self):
        gain = self.gain(4, self.width)

        def step(index, totals):
            at = rows_at(index, self.chunk)
            inv = self.stat(at, 5)
            normed = (self.resid[at, :] - self.stat(at, 4)) * inv
            upstream = self.pre[at, :]
            d_resid = self.d_mlp[at, :].astype(F32) + norm_back(upstream, normed, inv, gain)
            self.d_resid[at, :] = d_resid
            self.d_attn[at, :] = d_resid.astype(BF16)
            return (
                totals[0] + fold(upstream * normed),
                totals[1] + fold(upstream),
                totals[2] + fold(d_resid),
            )

        blank = jnp.zeros((8, self.width), F32)
        totals = lax.fori_loop(0, self.steps, step, (blank, blank, blank))
        for row, total in zip((5, 6, 4), totals):
            self.put_sum(row, total)

    def proj_back(self):
        size = self.width // self.gp.shape[0]
        product = dot_rows(self.att[...], self.d_attn[...])
        for index in range(self.gp.shape[0]):
            put_blocks(self.gp, index, product[index * size : (index + 1) * size])
        self.att[...] = dot_cols(self.d_attn[...], self.wp[...]).astype(BF16)
        self.d_bias[...] = jnp.zeros_like(self.d_bias)

    def attend_back(self, first, last, together=2):
        def step(index):
            top = last - 1 - index * together
            windows = [top - less for less in range(together)]
            attention_backward(windows, self.qkv, self.att, self.probs, self.d_bias, self.qkv)

        each((last - first) // together, step)

    def bias_back(self):
        self.put_table(reduce_bias(self.d_bias, self.spread, self.heads))
        ones = jnp.full((8, self.rows), 1.0, BF16)
        self.put_sum(8, dot(ones, self.qkv[0]), True)
        self.put_sum(9, dot(ones, self.qkv[2]), True)

    def qkv_weight_back(self):
        for part in range(3):
            put_columns(self.gqkv, part, dot_rows(self.attn_in[...], self.qkv[part]))

    def qkv_back(self):
        self.pre[...] = (
            dot_cols(self.qkv[0], self.wqkv[0])
            + dot_cols(self.qkv[1], self.wqkv[1])
            + dot_cols(self.qkv[2], self.wqkv[2])
        )

    def attn_back(self):
        gain = self.gain(2, self.width)

        def step(index, totals):
            at = rows_at(index, self.chunk)
            inv = self.stat(at, 3)
            normed = (self.section[at, :].astype(F32) - self.stat(at, 2)) * inv
            upstream = self.pre[at, :]
            d_section = self.d_resid[at, :] + norm_back(upstream, normed, inv, gain)
            self.d_mlp[at, :] = d_section.astype(BF16)
            return totals[0] + fold(upstream * normed), totals[1] + fold(upstream)

        blank = jnp.zeros((8, self.width), F32)
        totals = lax.fori_loop(0, self.steps, step, (blank, blank))
        self.put_sum(2, totals[0])
        self.put_sum(3, totals[1])

    def merge_weight_back(self):
        put_columns(self.gm, 0, dot_rows(self.merged[...], self.d_mlp[...]))

    def merge_in_back(self):
        for half, ref in enumerate((self.pre, self.d_resid)):
            rows = slice(half * self.width, (half + 1) * self.width)
            ref[...] = dot_cols(self.d_mlp[...], self.wm[rows, :])

    def merge_back(self, first, last, totals=None):
        gain = self.gain(0, self.wide)

        def step(index, totals):
            at = pl.ds(first * 16, (last - first) * 16)
            inv = self.stat(at, 1)
            normed = (self.x[at, :].astype(F32) - self.stat(at, 0)) * inv
            upstream = jnp.concatenate([self.pre[at, :], self.d_resid[at, :]], axis=1)
            self.d_in[at, :] = norm_back(upstream, normed, inv, gain)
            return totals[0] + fold(upstream * normed), totals[1] + fold(upstream)

        blank = jnp.zeros((8, self.wide), F32)
        totals = step(0, totals or (blank, blank))
        if last == self.rows // 16:
            self.put_sum(0, totals[0])
            self.put_sum(1, totals[1])
        return totals

    def put_sum(self, row, values, summed=False):
        values = values[0:1] if summed else sum_rows(values)
        place, ref = SUM_ROWS[row], self.late
        if place >= LATE_ROWS:
            place, ref = place - LATE_ROWS, self.early
        for block in range(values.shape[1] // LANES):
            lanes = slice(block * LANES, (block + 1) * LANES)
            ref[place + block : place + block + 1, :] = values[:, lanes]

    def put_up_sum(self, index, total):
        values = sum_rows(total)
        blocks = self.tile // LANES
        for block in range(blocks):
            place = SUM_ROWS[10] - LATE_ROWS + index * blocks + block
            self.early[pl.ds(place, 1), :] = values[:, block * LANES : (block + 1) * LANES]

    def put_table(self, values):
        for half in range(2):
            place = SUM_ROWS[11] - LATE_ROWS + half * self.heads
            lanes = slice(half * LANES, (half + 1) * LANES)
            self.early[place : place + self.heads, :] = values[:, lanes]


SUM_ROWS = (0, 8, 16, 20, 24, 28, 32, 36, 40, 44, 48, 64)
LATE_ROWS = 16
SUM_SIZE = 96


def put_blocks(ref, shard, values):
    rows = values.shape[0]
    for block in range(values.shape[1] // LANES):
        at = pl.ds(block * rows, rows)
        ref[shard, at, :] = values[:, block * LANES : (block + 1) * LANES].astype(BF16)


def put_columns(ref, part, values):
    rows = values.shape[0]
    for shard in range(ref.shape[0]):
        piece = values[:, shard * LANES : (shard + 1) * LANES]
        ref[shard, part * rows : (part + 1) * rows, :] = piece.astype(BF16)


def local_scratch(rows, wide, width, units):
    heads = width // HD
    windows = rows // TOK
    return dict(
        merged=pltpu.VMEM((rows, wide), BF16),
        section=pltpu.VMEM((rows, width), BF16),
        attn_in=pltpu.VMEM((rows, width), BF16),
        qkv=pltpu.VMEM((3, rows, width), BF16),
        probs=pltpu.VMEM((windows, SPAN, heads * SPAN), BF16),
        att=pltpu.VMEM((rows, width), BF16),
        resid=pltpu.VMEM((rows, width), F32),
        mlp_in=pltpu.VMEM((rows, width), BF16),
        hidden=pltpu.VMEM((rows, units), BF16),
        slope=pltpu.VMEM((rows, units), BF16),
        pre=pltpu.VMEM((rows, width), F32),
        d_mlp=pltpu.VMEM((rows, width), BF16),
        d_pre=pltpu.VMEM((rows, units), BF16),
        d_attn=pltpu.VMEM((rows, width), BF16),
        d_resid=pltpu.VMEM((rows, width), F32),
        gains=pltpu.VMEM((8, wide), F32),
        stats=pltpu.VMEM((rows, 8), F32),
        bias=pltpu.VMEM((SPAN, heads * SPAN), F32),
        d_bias=pltpu.VMEM((SPAN, heads * SPAN), F32),
        spread=pltpu.VMEM((SPAN * heads, LANES), F32),
    )


MESH_ID = pl.DeviceIdType.MESH


class Links:
    def __init__(self, send_sems, recv_sems):
        self.send_sems, self.recv_sems = send_sems, recv_sems
        self.slots, self.sent = {}, []
        self.sp, self.tp = lax.axis_index("sp"), lax.axis_index("tp")

    def slot(self, label):
        return self.slots.setdefault(label, len(self.slots))

    def place(self, way):
        over_tp, distance = way
        if over_tp:
            return self.sp, self.tp ^ distance
        return self.sp ^ distance, self.tp

    def copy(self, label, way, source, target):
        slot = self.slot(label)
        return pltpu.make_async_remote_copy(
            src_ref=source,
            dst_ref=target,
            send_sem=self.send_sems.at[slot],
            recv_sem=self.recv_sems.at[slot],
            device_id=self.place(way),
            device_id_type=MESH_ID,
        )

    def send(self, label, way, source, target):
        copy = self.copy(label, way, source, target)
        copy.start()
        self.sent.append(copy)

    def receive(self, label, way, target):
        self.copy(label, way, target, target).wait_recv()

    def keep(self, label, source, target):
        copy = pltpu.make_async_copy(source, target, self.recv_sems.at[self.slot(label)])
        copy.start()
        return copy

    def greet(self, ways):
        barrier = pltpu.get_barrier_semaphore()
        for way in ways:
            pl.semaphore_signal(
                barrier, inc=1, device_id=self.place(way), device_id_type=MESH_ID
            )
        pl.semaphore_wait(barrier, len(ways))

    def drain(self):
        for copy in self.sent:
            copy.wait_send()


CORE, ACROSS, BESIDE = (True, 1), (True, 2), (False, 1)


def far(step):
    return False, 2 * step


class Gather:
    def __init__(self, links, label, own, whole, view, split=True):
        self.links, self.name, self.own, self.whole = links, label, own, whole
        self.view, self.split = view, split
        self.half = links.sp & 1 if split else None

    def part(self, shard, half=None):
        return self.view(self.whole, shard, half)

    def label(self, step):
        return self.name, step

    def start(self):
        links = self.links
        mine = links.tp
        source = self.view(self.own, None, None)
        self.local = links.keep(self.label(0), source, self.part(mine))
        links.send(
            self.label(1), ACROSS, self.view(self.own, None, self.half),
            self.part(mine, self.half),
        )
        links.send(self.label(2), CORE, source, self.part(mine))

    def forward(self):
        links = self.links
        block = self.part(links.tp ^ 2, self.half)
        links.receive(self.label(1), ACROSS, block)
        if self.split:
            links.send(self.label(3), BESIDE, block, block)
        links.send(self.label(4), CORE, block, block)

    def beside(self):
        links = self.links
        block = self.part(links.tp ^ 2, 1 - self.half)
        links.receive(self.label(3), BESIDE, block)
        links.send(self.label(5), CORE, block, block)

    def finish(self):
        links = self.links
        self.local.wait()
        links.receive(self.label(2), CORE, self.part(links.tp ^ 1))
        links.receive(self.label(4), CORE, self.part(links.tp ^ 3, self.half))
        if self.split:
            links.receive(self.label(5), CORE, self.part(links.tp ^ 3, 1 - self.half))


def column_view(size, first, rows):
    def view(ref, shard, half):
        start, count = (first, rows) if half is None else (first + half * (rows // 2), rows // 2)
        at = pl.ds(start if half is None else pl.multiple_of(start, 16), count)
        if shard is None:
            return ref.at[at, :]
        return ref.at[at, pl.ds(pl.multiple_of(shard * size, LANES), size)]

    return view


def row_view(size, first, rows):
    def view(ref, shard, half):
        start = first if shard is None else shard * size + first
        if half is None:
            return ref.at[pl.ds(start if shard is None else pl.multiple_of(start, 16), rows), :]
        return ref.at[pl.ds(pl.multiple_of(start + half * (rows // 2), 16), rows // 2), :]

    return view


def lead_view(ref, shard, half):
    return ref if shard is None else ref.at[shard]


def add_rows(target, start, rows, terms, chunk=512):
    chunk = math.gcd(rows, chunk)

    def step(index):
        offset = index * chunk

        def at(first):
            return pl.ds(pl.multiple_of(first + offset, 16), chunk)

        total = None
        for ref, first in terms:
            value = ref[at(first), :].astype(F32)
            total = value if total is None else total + value
        target[at(start), :] = total.astype(target.dtype)

    each(rows // chunk, step)


class Reduce:
    def __init__(self, links, label, grads, core_in, first_in, second_in, far_in, result, group,
                 across_first):
        self.links, self.name, self.grads = links, label, grads
        self.core_in, self.first_in, self.second_in = core_in, first_in, second_in
        self.far_in, self.result, self.group = far_in, result, group
        self.rows = grads.shape[1]
        self.half_rows = self.rows // 2
        self.piece = self.half_rows // group
        self.half = links.sp & 1
        self.seat = links.sp >> 1
        self.across = links.tp >> 1
        if across_first:
            self.add, self.first = self.core_add_across, self.across_beside
            self.second = self.beside_last
        else:
            self.add, self.first = self.core_add_beside, self.beside_across
            self.second = self.across_last

    def label(self, *step):
        return (self.name,) + step

    def rows_of(self, ref, half, piece=None):
        if piece is None:
            return ref.at[pl.ds(pl.multiple_of(half * self.half_rows, 16), self.half_rows), :]
        start = half * self.half_rows + piece * self.piece
        return ref.at[pl.ds(pl.multiple_of(start, 16), self.piece), :]

    def core_send(self, across, step):
        shard = (self.links.tp & 1) ^ 1 | 2 * across
        self.links.send(
            self.label(step), CORE, self.grads.at[shard], self.core_in.at[across]
        )

    def far(self):
        self.core_send(self.across ^ 1, 0)

    def near(self):
        self.core_send(self.across, 1)

    def receive_far(self):
        self.links.receive(self.label(0), CORE, self.core_in.at[self.across ^ 1])

    def receive_near(self):
        self.links.receive(self.label(1), CORE, self.core_in.at[self.across])

    def core_add_across(self):
        self.receive_far()
        other = self.links.tp ^ 2
        block = self.grads.at[other]
        add_rows(block, 0, self.rows, [(block, 0), (self.core_in.at[self.across ^ 1], 0)])
        self.links.send(self.label(2), ACROSS, block, self.first_in)

    def across_beside(self):
        links = self.links
        self.receive_near()
        links.receive(self.label(2), ACROSS, self.first_in)
        block = self.grads.at[links.tp]
        terms = [(block, 0), (self.core_in.at[self.across], 0), (self.first_in, 0)]
        add_rows(block, 0, self.rows, terms)
        links.send(
            self.label(3), BESIDE, self.rows_of(block, 1 - self.half), self.second_in
        )

    def beside_last(self):
        self.links.receive(self.label(3), BESIDE, self.second_in)
        self.add_and_spread([(self.second_in, 0)])

    def core_add_beside(self):
        links = self.links
        self.receive_far()
        self.receive_near()
        for across in range(2):
            block = self.grads.at[(links.tp & 1) | 2 * across]
            add_rows(block, 0, self.rows, [(block, 0), (self.core_in.at[across], 0)])
            links.send(
                self.label(3, across), BESIDE, self.rows_of(block, 1 - self.half),
                self.first_in.at[across],
            )

    def beside_across(self):
        links = self.links
        for across in range(2):
            links.receive(self.label(3, across), BESIDE, self.first_in.at[across])
        block = self.grads.at[links.tp ^ 2]
        mine = self.half * self.half_rows
        terms = [(block, mine), (self.first_in.at[self.across ^ 1], 0)]
        add_rows(block, mine, self.half_rows, terms)
        links.send(self.label(2), ACROSS, self.rows_of(block, self.half), self.second_in)

    def across_last(self):
        self.links.receive(self.label(2), ACROSS, self.second_in)
        self.add_and_spread([(self.first_in.at[self.across], 0), (self.second_in, 0)])

    def add_and_spread(self, terms):
        block = self.grads.at[self.links.tp]
        mine = self.half * self.half_rows
        add_rows(block, mine, self.half_rows, [(block, mine)] + terms)
        for step in range(1, self.group):
            self.links.send(
                self.label(4, step), far(step),
                self.rows_of(block, self.half, self.seat ^ step), self.far_in.at[step - 1],
            )

    def spread(self):
        links = self.links
        block = self.grads.at[links.tp]
        mine = self.half * self.half_rows + self.seat * self.piece
        terms = [(block, mine)]
        for step in range(1, self.group):
            links.receive(self.label(4, step), far(step), self.far_in.at[step - 1])
            terms.append((self.far_in.at[step - 1], 0))
        add_rows(self.result, mine, self.piece, terms)
        done = self.rows_of(self.result, self.half, self.seat)
        for step in range(1, self.group):
            links.send(self.label(5, step), far(step), done, done)

    def back(self):
        links = self.links
        for step in range(1, self.group):
            links.receive(
                self.label(5, step), far(step),
                self.rows_of(self.result, self.half, self.seat ^ step),
            )
        done = self.rows_of(self.result, self.half)
        links.send(self.label(6), BESIDE, done, done)

    def last(self):
        self.links.receive(
            self.label(6), BESIDE, self.rows_of(self.result, 1 - self.half)
        )


class Total:
    def __init__(self, links, label, stages, inboxes, seats, result):
        self.links, self.name, self.stages, self.inboxes = links, label, stages, inboxes
        self.seats, self.result = seats, result
        self.group = seats.shape[0]
        self.seat = links.sp >> 1

    def exchange(self, stage, way):
        self.links.send((self.name, stage), way, self.stages.at[stage], self.inboxes.at[stage])

    def take(self, stage, way):
        self.links.receive((self.name, stage), way, self.inboxes.at[stage])
        return self.stages[stage] + self.inboxes[stage]

    def send(self):
        self.exchange(0, CORE)

    def core(self):
        self.stages[1] = self.take(0, CORE)
        self.exchange(1, ACROSS)

    def across(self):
        self.stages[2] = self.take(1, ACROSS)
        self.exchange(2, BESIDE)

    def beside(self):
        mine = self.seats.at[self.seat]
        mine[...] = self.take(2, BESIDE)
        for step in range(1, self.group):
            self.links.send((self.name, 3, step), far(step), mine, mine)

    def last(self):
        for step in range(1, self.group):
            self.links.receive((self.name, 3, step), far(step), self.seats.at[self.seat ^ step])
        total = self.seats[0]
        for seat in range(1, self.group):
            total = total + self.seats[seat]
        self.result[...] = total


def schedule(local, g, u, done):
    windows = local.windows
    tiles = local.tiles()

    def attend_back(first, last):
        local.attend_back(windows - last * windows // 8, windows - first * windows // 8)

    local.begin()
    local.merge_norm()
    local.prepare()
    local.grad_rows()
    g.pack.forward()
    g.wm0.forward()
    g.wm1.forward()
    g.wq.forward()
    g.wm0.beside()
    g.wk.forward()
    g.wm0.finish()
    g.wm1.beside()
    g.wv.forward()
    g.wm1.finish()
    local.merge()
    g.wq.beside()
    g.wp.forward()
    g.pack.finish()
    local.table_bias()
    g.wk.beside()
    g.wu0.forward()
    local.attn_norm()
    g.wv.beside()
    g.wq.finish()
    local.project(0)
    g.wu1.forward()
    g.wk.finish()
    local.project(1)
    g.wv.finish()
    local.project(2)
    g.wp.beside()
    g.wu2.forward()
    local.attend(0, windows // 4)
    g.wu0.beside()
    g.wu3.forward()
    local.attend(windows // 4, windows // 2)
    g.wu1.beside()
    local.attend(windows // 2, 3 * windows // 4)
    g.wu2.beside()
    g.wd0.forward()
    local.attend(3 * windows // 4, windows)
    g.wu3.beside()
    g.wp.finish()
    local.attn_out()
    g.wd1.forward()
    local.mlp_norm()
    g.wu0.finish()
    g.wu1.finish()
    g.wu2.finish()
    g.wu3.finish()
    local.up(tiles[0])
    g.wd0.beside()
    u.gd0.far()
    u.gd1.far()
    local.up(tiles[1])
    g.wd1.beside()
    u.gd0.add()
    local.up(tiles[2])
    u.gd0.near()
    u.gd1.near()
    local.up(tiles[3])
    u.gd1.add()
    g.wd0.finish()
    g.wd1.finish()
    local.hidden_back(tiles[0])
    u.gu0.far()
    u.gu1.far()
    local.hidden_back_pair()
    u.gu1.add()
    u.gu0.add()
    u.gd0.first()
    u.gu0.near()
    u.gu1.near()
    local.hidden_back(tiles[3])
    local.up_back()
    u.gd1.first()
    local.mlp_back()
    local.proj_back()
    u.gd0.second()
    u.gp0.far()
    u.gp0.near()
    attend_back(0, 2)
    u.gu1.first()
    u.gp0.add()
    attend_back(2, 4)
    attend_back(4, 6)
    u.gu0.first()
    u.gd0.spread()
    attend_back(6, 8)
    u.gu1.second()
    local.qkv_weight_back()
    u.gd1.second()
    u.gp0.first()
    u.qkv0.far()
    u.qkv0.near()
    u.qkv1.far()
    u.qkv1.near()
    u.qkv2.far()
    u.qkv2.near()
    local.qkv_back()
    u.gd0.back()
    u.gu0.second()
    u.qkv1.add()
    u.qkv0.add()
    u.qkv2.add()
    local.attn_back()
    u.gp0.second()
    local.merge_weight_back()
    u.gu1.spread()
    u.gm0.far()
    u.gm0.near()
    u.gm1.far()
    u.gm1.near()
    local.down()
    u.gm0.add()
    u.gd1.spread()
    u.gm1.add()
    u.qkv0.first()
    u.qkv1.first()
    u.qkv2.first()
    u.gu0.spread()
    u.gp0.spread()
    local.finish()
    done.out()
    local.merge_in_back()
    u.gm0.first()
    u.gm1.first()
    u.gu1.back()
    part = local.rows // 16 // 7
    totals = local.merge_back(0, 2 * part)
    u.qkv1.second()
    u.qkv0.second()
    totals = local.merge_back(2 * part, 5 * part, totals)
    local.merge_back(5 * part, 7 * part, totals)
    done.d_in()
    u.late.send()
    u.qkv2.second()
    local.bias_back()
    u.early.send()
    u.gd1.back()
    u.late.core()
    u.gm0.second()
    u.gm1.second()
    u.early.core()
    u.gu0.back()
    u.gp0.back()
    u.late.across()
    u.qkv1.spread()
    u.early.across()
    u.qkv0.spread()
    u.gm0.spread()
    u.qkv2.spread()
    u.gm1.spread()
    u.late.beside()
    u.early.beside()
    u.qkv1.back()
    u.qkv0.back()
    u.gm0.back()
    u.qkv2.back()
    u.gm1.back()
    u.gd0.last()
    u.gu1.last()
    u.gd1.last()
    u.gu0.last()
    u.gp0.last()
    u.qkv1.last()
    u.qkv0.last()
    u.late.last()
    u.gm0.last()
    u.qkv2.last()
    u.gm1.last()
    u.early.last()


SHARDS = 4
PIECES = 7


class Refs:
    def __init__(self, names, refs):
        self.__dict__.update(zip(names, refs, strict=True))


UNITS = dict(
    gd0=(0, 1024, True),
    gd1=(1024, 1024, False),
    gu0=(0, 1024, True),
    gu1=(1024, 1024, True),
    gp0=(0, 512, False),
    qkv0=(0, 512, True),
    qkv1=(512, 512, False),
    qkv2=(1024, 512, True),
    gm0=(0, 512, True),
    gm1=(512, 512, False),
)


def fill_pack(pack, rel, qv, ub):
    pack[...] = jnp.zeros_like(pack)
    pack[0 : rel.shape[0], 0:REL] = rel[...].astype(F32)
    pack[4:6, 0:LANES] = qv[...].astype(F32)
    for block in range(ub.shape[0]):
        lanes = slice(block * LANES, (block + 1) * LANES)
        pack[6:7, lanes] = ub[block : block + 1, :].astype(F32)


def gathers_of(links, r):
    wide, here = r.own_wm.shape
    width, tile = r.own_wu.shape
    columns = functools.partial(column_view, here)
    up = functools.partial(column_view, tile)
    down = functools.partial(row_view, tile)
    parts = dict(
        pack=(r.pack, r.packs, lead_view, False),
        wm0=(r.own_wm, r.wm, columns(0, wide // 2)),
        wm1=(r.own_wm, r.wm, columns(wide // 2, wide // 2)),
        wq=(r.own_wqkv.at[0], r.wqkv.at[0], columns(0, width)),
        wk=(r.own_wqkv.at[1], r.wqkv.at[1], columns(0, width)),
        wv=(r.own_wqkv.at[2], r.wqkv.at[2], columns(0, width)),
        wp=(r.own_wp, r.wp, row_view(here, 0, here)),
        wu0=(r.own_wu, r.wu, up(0, width // 4)),
        wu1=(r.own_wu, r.wu, up(width // 4, width // 4)),
        wu2=(r.own_wu, r.wu, up(width // 2, width // 4)),
        wu3=(r.own_wu, r.wu, up(3 * width // 4, width // 4)),
        wd0=(r.own_wd, r.wd, down(0, tile // 2)),
        wd1=(r.own_wd, r.wd, down(tile // 2, tile // 2)),
    )
    made = [Gather(links, label, *part) for label, part in enumerate(parts.values())]
    return Refs(parts, made)


def reduces_of(links, r, boxes, first_label):
    grads = (r.gd, r.gd, r.gu, r.gu, r.gp, r.gqkv, r.gqkv, r.gqkv, r.gm, r.gm)
    results = (r.rd, r.rd, r.ru, r.ru, r.rp, r.rqkv, r.rqkv, r.rqkv, r.rm, r.rm)
    made = []
    for index, (first, size, across_first) in enumerate(UNITS.values()):
        at = pl.ds(first, size)
        group = boxes[index][3].shape[0] + 1
        made.append(
            Reduce(
                links, first_label + index, grads[index].at[:, at, :], *boxes[index],
                results[index].at[at, :], group, across_first,
            )
        )
    return Refs(UNITS, made)


def whole_kernel(names, group, *refs):
    boxes = refs[len(names) :]
    r = Refs(names, refs[: len(names)])
    links = Links(r.send_sems, r.recv_sems)
    arriving = [links.keep((-1, 0), r.h_x, r.x), links.keep((-1, 1), r.h_grad_out, r.grad_out)]
    fill_pack(r.pack, r.rel, r.qv, r.ub)
    links.greet([CORE, ACROSS, BESIDE] + [far(step) for step in range(1, group)])
    g = gathers_of(links, r)
    for gather in vars(g).values():
        gather.start()
    u = reduces_of(links, r, [boxes[4 * unit : 4 * unit + 4] for unit in range(len(UNITS))], 100)
    late, early = pl.ds(0, LATE_ROWS), pl.ds(LATE_ROWS, SUM_SIZE - LATE_ROWS)
    u.late = Total(links, 200, r.late_stages, r.late_in, r.late_seats, r.sums.at[late, :])
    u.early = Total(links, 201, r.early_stages, r.early_in, r.early_seats, r.sums.at[early, :])
    here = r.rel.shape[0]

    def table():
        parts = [r.packs[shard, 0:here, : 2 * LANES] for shard in range(SHARDS)]
        return jnp.concatenate(parts, axis=0)

    def qkv_bias(part):
        row = 4 if part == 0 else 5
        parts = [r.packs[shard, row : row + 1, :LANES] for shard in range(SHARDS)]
        return jnp.concatenate(parts, axis=1)

    def up_bias(index):
        return r.packs[index, 6:7, :]

    vectors = (
        r.merge_gain, r.merge_bias, r.attn_gain, r.attn_bias, r.mlp_gain, r.mlp_bias, r.proj_bias,
        r.down_bias,
    )
    fields = dict(
        vars(r), table=table, qkv_bias=qkv_bias, up_bias=up_bias, vectors=vectors,
        arriving=arriving, early=r.early_stages.at[0], late=r.late_stages.at[0],
    )
    local = Local(fields, links.tp * (r.x.shape[0] // TOK))
    leaving = []

    def put_d_in():
        leaving.append(links.keep((-1, 2), r.d_in, r.h_d_in))

    def put_out():
        leaving.append(links.keep((-1, 3), r.out, r.h_out))

    schedule(local, g, u, Refs(dict(d_in=0, out=0), (put_d_in, put_out)))
    for copy in leaving:
        copy.wait()
    links.drain()


def wide_rows(result, out):
    rows = out.shape[0]
    for block in range(out.shape[1] // LANES):
        lanes = slice(block * LANES, (block + 1) * LANES)
        out[:, lanes] = result[block * rows : (block + 1) * rows, :].astype(F32)


def finish_kernel(names, *refs):
    r = Refs(names, refs)
    tp = lax.axis_index("tp")
    pieces = []
    for source, target, held in ((r.h_d_in, r.o_d_in, r.v_d_in), (r.h_out, r.o_out, r.v_out)):
        size = held.shape[0] // PIECES
        for index in range(PIECES):
            at = pl.ds(index * size, size)
            number = 2 * len(pieces)
            pieces.append(
                (
                    pltpu.make_async_copy(source.at[at], held.at[at], r.sems.at[number]),
                    pltpu.make_async_copy(held.at[at], target.at[at], r.sems.at[number + 1]),
                )
            )
    for incoming, _ in pieces:
        incoming.start()
    vectors = (
        r.o_merge_gain, r.o_merge_bias, r.o_attn_gain, r.o_attn_bias, r.o_proj_bias, r.o_mlp_gain,
        r.o_mlp_bias, r.o_down_bias,
    )
    for row, out in enumerate(vectors):
        out[...] = r.sums[SUM_ROWS[row] : SUM_ROWS[row] + out.shape[0], :]
    for index in range(2):
        r.o_qv[index : index + 1, :] = r.sums[pl.ds(SUM_ROWS[8 + index] + tp, 1), :]
    blocks = r.o_ub.shape[0]
    for index in range(blocks):
        place = pl.ds(SUM_ROWS[10] + tp * blocks + index, 1)
        r.o_ub[index : index + 1, :] = r.sums[place, :]
    mine = r.o_rel.shape[0]
    for index in range(mine):
        first = SUM_ROWS[11] + tp * mine + index
        low, high = r.sums[pl.ds(first, 1), :], r.sums[pl.ds(first + SHARDS * mine, 1), :]
        r.o_rel[index : index + 1, :LANES] = low
        r.o_rel[index : index + 1, LANES:] = high[:, : REL - LANES]
    for incoming, outgoing in pieces:
        incoming.wait()
        outgoing.start()
    for result, out in ((r.rp, r.o_gp), (r.ru, r.o_gu), (r.rd, r.o_gd), (r.rm, r.o_gm)):
        wide_rows(result, out)
    rows = r.o_gqkv.shape[1]
    for part in range(r.o_gqkv.shape[0]):
        r.o_gqkv[part] = r.rqkv[part * rows : (part + 1) * rows, :].astype(F32)
    for _, outgoing in pieces:
        outgoing.wait()


VMEM_SPEC = pl.BlockSpec(memory_space=pltpu.VMEM)
SMEM_SPEC = pl.BlockSpec(memory_space=pltpu.SMEM)
HBM_SPEC = pl.BlockSpec(memory_space=pl.ANY)


def whole_call(group, small, large):
    rows, wide = large["h_x"].shape
    width, tile = large["own_wu"].shape
    units = SHARDS * tile
    scratch = local_scratch(rows, wide, width, units)
    block = lambda *shape: pltpu.VMEM(shape, BF16)
    exact = lambda *shape: pltpu.VMEM(shape, F32)
    early = SUM_SIZE - LATE_ROWS
    count = 13 * 6 + len(UNITS) * (6 + 2 * group) + 2 * (3 + group) + 4
    scratch.update(
        wm=block(wide, width), wqkv=block(3, width, width), wp=block(width, width),
        wu=block(width, units), wd=block(units, width), pack=exact(8, tile),
        packs=exact(SHARDS, 8, tile), x=block(rows, wide), grad_out=block(rows, width),
        out=block(rows, width), d_in=exact(rows, wide), gd=block(SHARDS, units, LANES),
        gu=block(SHARDS, units, LANES), gp=block(SHARDS, width, LANES),
        gqkv=block(SHARDS, 3 * width, LANES), gm=block(SHARDS, wide, LANES),
        late_stages=exact(3, LATE_ROWS, LANES), late_in=exact(3, LATE_ROWS, LANES),
        late_seats=exact(group, LATE_ROWS, LANES), early_stages=exact(3, early, LANES),
        early_in=exact(3, early, LANES), early_seats=exact(group, early, LANES),
        send_sems=pltpu.SemaphoreType.DMA((count,)), recv_sems=pltpu.SemaphoreType.DMA((count,)),
    )
    boxes = []
    for _, size, across_first in UNITS.values():
        half = size // 2
        boxes += [
            block(2, size, LANES),
            block(size, LANES) if across_first else block(2, half, LANES),
            block(half, LANES),
            block(group - 1, half // group, LANES),
        ]
    result = lambda size: jax.ShapeDtypeStruct((size, LANES), BF16)
    outs = dict(
        h_out=jax.ShapeDtypeStruct((rows, width), BF16),
        h_d_in=jax.ShapeDtypeStruct((rows, wide), F32),
        rd=result(units), ru=result(units), rp=result(width), rqkv=result(3 * width),
        rm=result(wide), sums=jax.ShapeDtypeStruct((SUM_SIZE, LANES), F32),
    )
    names = tuple(small) + tuple(large) + tuple(outs) + tuple(scratch)
    made = pl.pallas_call(
        functools.partial(whole_kernel, names, group),
        out_shape=list(outs.values()),
        in_specs=[SMEM_SPEC] * 2 + [VMEM_SPEC] * (len(small) - 2) + [HBM_SPEC] * len(large),
        out_specs=[HBM_SPEC] * 2 + [VMEM_SPEC] * (len(outs) - 2),
        scratch_shapes=list(scratch.values()) + boxes,
        compiler_params=pltpu.CompilerParams(
            vmem_limit_bytes=63 * MIB, collective_id=0, has_side_effects=True
        ),
    )(*small.values(), *large.values())
    return dict(zip(outs, made, strict=True))


def finish_call(results, shapes):
    (rows, width), (_, wide) = shapes["o_out"].shape, shapes["o_d_in"].shape
    scratch = dict(
        v_out=pltpu.VMEM((rows, width), BF16), v_d_in=pltpu.VMEM((rows, wide), F32),
        sems=pltpu.SemaphoreType.DMA((4 * PIECES,)),
    )
    names = tuple(results) + tuple(shapes) + tuple(scratch)
    made = pl.pallas_call(
        functools.partial(finish_kernel, names),
        out_shape=list(shapes.values()),
        in_specs=[HBM_SPEC] * 2 + [VMEM_SPEC] * (len(results) - 2),
        out_specs=[HBM_SPEC] * 2 + [VMEM_SPEC] * (len(shapes) - 2),
        scratch_shapes=list(scratch.values()),
        compiler_params=pltpu.CompilerParams(vmem_limit_bytes=63 * MIB),
    )(*results.values())
    return Refs(shapes, made)


def on_device(
    inputs, grad_out, window_valid, window_edge, merge_gain, merge_bias, merge_weight, attn_gain,
    attn_bias, query_key_value_weight, qv_bias, rel_table, proj_weight, proj_bias, mlp_gain,
    mlp_bias, up_weight, up_bias, down_weight, down_bias,
):
    lines = lambda vector: vector.reshape(-1, LANES)
    small = dict(
        valid=window_valid, edge=window_edge, rel=rel_table.T, qv=qv_bias, ub=lines(up_bias),
        merge_gain=lines(merge_gain), merge_bias=lines(merge_bias), attn_gain=lines(attn_gain),
        attn_bias=lines(attn_bias), mlp_gain=lines(mlp_gain), mlp_bias=lines(mlp_bias),
        proj_bias=lines(proj_bias), down_bias=lines(down_bias),
    )
    qkv = jnp.transpose(query_key_value_weight, (1, 0, 2))
    large = dict(
        h_x=inputs, h_grad_out=grad_out, own_wm=merge_weight, own_wqkv=qkv, own_wp=proj_weight,
        own_wu=up_weight, own_wd=down_weight,
    )
    results = whole_call(lax.axis_size("sp") // 2, small, large)
    like = lambda array: jax.ShapeDtypeStruct(array.shape, F32)
    shapes = dict(
        o_out=jax.ShapeDtypeStruct(grad_out.shape, BF16), o_d_in=like(inputs),
        o_gm=like(merge_weight), o_gqkv=like(qkv), o_gp=like(proj_weight), o_gu=like(up_weight),
        o_gd=like(down_weight), o_qv=like(qv_bias), o_rel=like(rel_table.T),
        o_ub=like(lines(up_bias)), o_merge_gain=like(lines(merge_gain)),
        o_merge_bias=like(lines(merge_bias)), o_attn_gain=like(lines(attn_gain)),
        o_attn_bias=like(lines(attn_bias)), o_proj_bias=like(lines(proj_bias)),
        o_mlp_gain=like(lines(mlp_gain)), o_mlp_bias=like(lines(mlp_bias)),
        o_down_bias=like(lines(down_bias)),
    )
    done = finish_call(results, shapes)
    flat = lambda block: block.reshape(-1)
    return (
        done.o_out, done.o_d_in, flat(done.o_merge_gain), flat(done.o_merge_bias), done.o_gm,
        flat(done.o_attn_gain), flat(done.o_attn_bias), jnp.transpose(done.o_gqkv, (1, 0, 2)),
        done.o_qv, done.o_rel.T, done.o_gp, flat(done.o_proj_bias), flat(done.o_mlp_gain),
        flat(done.o_mlp_bias), done.o_gu, flat(done.o_ub), done.o_gd, flat(done.o_down_bias),
    )


def solution(mesh):
    placed = (
        P(("sp", "tp"), None),
        P(("sp", "tp"), None),
        P("sp"),
        P("sp"),
        P(),
        P(),
        P(None, "tp"),
        P(),
        P(),
        P(None, None, "tp"),
        P(None, "tp"),
        P(None, "tp"),
        P("tp", None),
        P(),
        P(),
        P(),
        P(None, "tp"),
        P("tp"),
        P("tp", None),
        P(),
    )
    return jax.shard_map(
        on_device,
        mesh=mesh,
        in_specs=placed,
        out_specs=(
            P(("sp", "tp"), None),
            P(("sp", "tp"), None),
            P(),
            P(),
            P(None, "tp"),
            P(),
            P(),
            P(None, None, "tp"),
            P(None, "tp"),
            P(None, "tp"),
            P("tp", None),
            P(),
            P(),
            P(),
            P(None, "tp"),
            P("tp"),
            P("tp", None),
            P(),
        ),
        check_vma=False,
    )
```

profile of v0, /device:TPU:0, one launch (start us, length us, event | category | flops | bytes accessed | tf_op | source)
XLA Modules:
  0.0 115.3 jit_solution(1412693347193274144)
XLA Ops:
  0.7 107.7 %shard_map.331 = (bf16[784,512]{1,0:T(8,128)(2,1)}, f32[784,1024]{1,0:T(8,128)}, bf16[2048,128]{1,0:T(8,128)(2,1)}, bf16[2048,128]{1,0:T(8,128)(2,1)}, bf16[512,...) custom-call(s32[64]{0:T(128)} %refs_0_.1, s32[64]{0:T(128)} %refs_1_.1, ...), custom_call_target="tpu_custom_call" | custom-call | tf_op jit(solution)/shard_map/pallas_call | solution.py:1390
  108.4 6.7 %shard_map.332 = (bf16[784,512]{1,0:T(8,128)(2,1)}, f32[784,1024]{1,0:T(8,128)}, f32[1024,128]{1,0:T(8,128)}, f32[3,512,128]{2,1,0:T(8,128)}, f32[128,512]{1,0:T...) custom-call(bf16[784,512]{1,0:T(8,128)(2,1)} %get-tuple-element.44.r, ...), custom_call_target="tpu_custom_call" | custom-call | tf_op jit(solution)/shard_map/pallas_call | solution.py:1410
where the time goes:
time: 115 us
  Pallas kernels  114 us (99%)
    pallas_call x1, Pallas kernels, whole_call(): pl.pallas_call(functools.partial(whole_kernel, names, group), out_shape=l...  108 us
    pallas_call x1, Pallas kernels, finish_call(): pl.pallas_call(functools.partial(finish_kernel, names), out_shape=list(sh...  6.7 us

commit v1 on v0

--- a/solution.py
+++ b/solution.py
@@ -1060,9 +1060,9 @@
     u.gu0.far()
     u.gu1.far()
     local.hidden_back_pair()
+    u.gd0.first()
+    u.gu0.add()
     u.gu1.add()
-    u.gu0.add()
-    u.gd0.first()
     u.gu0.near()
     u.gu1.near()
     local.hidden_back(tiles[3])
@@ -1071,20 +1071,20 @@
     local.mlp_back()
     local.proj_back()
     u.gd0.second()
+    u.gu0.first()
     u.gp0.far()
     u.gp0.near()
     attend_back(0, 2)
-    u.gu1.first()
     u.gp0.add()
     attend_back(2, 4)
     attend_back(4, 6)
-    u.gu0.first()
+    u.gu0.second()
+    u.gu1.first()
     u.gd0.spread()
     attend_back(6, 8)
-    u.gu1.second()
+    u.gp0.first()
+    u.gd1.second()
     local.qkv_weight_back()
-    u.gd1.second()
-    u.gp0.first()
     u.qkv0.far()
     u.qkv0.near()
     u.qkv1.far()
@@ -1092,76 +1092,76 @@
     u.qkv2.far()
     u.qkv2.near()
     local.qkv_back()
-    u.gd0.back()
-    u.gu0.second()
+    u.gp0.second()
+    u.gu1.second()
+    u.qkv0.add()
     u.qkv1.add()
-    u.qkv0.add()
+    u.gu0.spread()
     u.qkv2.add()
     local.attn_back()
-    u.gp0.second()
     local.merge_weight_back()
-    u.gu1.spread()
+    u.gd0.back()
     u.gm0.far()
     u.gm0.near()
     u.gm1.far()
     u.gm1.near()
     local.down()
+    u.gd1.spread()
     u.gm0.add()
-    u.gd1.spread()
+    u.qkv1.first()
+    u.qkv0.first()
+    u.gp0.spread()
     u.gm1.add()
-    u.qkv0.first()
-    u.qkv1.first()
-    u.qkv2.first()
-    u.gu0.spread()
-    u.gp0.spread()
     local.finish()
     done.out()
     local.merge_in_back()
-    u.gm0.first()
-    u.gm1.first()
-    u.gu1.back()
+    u.qkv2.first()
+    u.gu1.spread()
     part = local.rows // 16 // 7
     totals = local.merge_back(0, 2 * part)
-    u.qkv1.second()
     u.qkv0.second()
     totals = local.merge_back(2 * part, 5 * part, totals)
     local.merge_back(5 * part, 7 * part, totals)
     done.d_in()
     u.late.send()
-    u.qkv2.second()
+    u.gm0.first()
+    u.gu0.back()
     local.bias_back()
     u.early.send()
+    u.qkv1.second()
+    u.gm1.first()
+    u.late.core()
+    u.qkv2.second()
     u.gd1.back()
-    u.late.core()
+    u.early.core()
     u.gm0.second()
+    u.gp0.back()
     u.gm1.second()
-    u.early.core()
-    u.gu0.back()
-    u.gp0.back()
+    u.gu1.back()
     u.late.across()
-    u.qkv1.spread()
     u.early.across()
     u.qkv0.spread()
+    u.qkv1.spread()
+    u.qkv2.spread()
     u.gm0.spread()
-    u.qkv2.spread()
     u.gm1.spread()
     u.late.beside()
     u.early.beside()
+    u.qkv0.back()
     u.qkv1.back()
-    u.qkv0.back()
+    u.qkv2.back()
     u.gm0.back()
-    u.qkv2.back()
     u.gm1.back()
     u.gd0.last()
+    u.gu0.last()
+    u.gd1.last()
+    u.gp0.last()
     u.gu1.last()
-    u.gd1.last()
-    u.gu0.last()
-    u.gp0.last()
+    u.qkv0.last()
     u.qkv1.last()
-    u.qkv0.last()
     u.late.last()
+    u.qkv2.last()
     u.gm0.last()
-    u.qkv2.last()
     u.gm1.last()
     u.early.last()
 

time: 115 us -> 116 us (level)
  no operation moved by 1% of the time
where the time goes in v1:
time: 116 us
  Pallas kernels  115 us (99%)
    pallas_call x1, Pallas kernels, whole_call(): pl.pallas_call(functools.partial(whole_kernel, names, group), out_shape=l...  108 us
    pallas_call x1, Pallas kernels, finish_call(): pl.pallas_call(functools.partial(finish_kernel, names), out_shape=list(sh...  6.7 us

profile of v1, /device:TPU:0, one launch (start us, length us, event | category | flops | bytes accessed | tf_op | source)
XLA Modules:
  0.0 116.0 jit_solution(688722863999439609)
XLA Ops:
  0.7 108.4 %shard_map.331 = (bf16[784,512]{1,0:T(8,128)(2,1)}, f32[784,1024]{1,0:T(8,128)}, bf16[2048,128]{1,0:T(8,128)(2,1)}, bf16[2048,128]{1,0:T(8,128)(2,1)}, bf16[512,...) custom-call(s32[64]{0:T(128)} %refs_0_.1, s32[64]{0:T(128)} %refs_1_.1, ...), custom_call_target="tpu_custom_call" | custom-call | tf_op jit(solution)/shard_map/pallas_call | solution.py:1390
  109.1 6.7 %shard_map.332 = (bf16[784,512]{1,0:T(8,128)(2,1)}, f32[784,1024]{1,0:T(8,128)}, f32[1024,128]{1,0:T(8,128)}, f32[3,512,128]{2,1,0:T(8,128)}, f32[128,512]{1,0:T...) custom-call(bf16[784,512]{1,0:T(8,128)(2,1)} %get-tuple-element.44.r, ...), custom_call_target="tpu_custom_call" | custom-call | tf_op jit(solution)/shard_map/pallas_call | solution.py:1410
